TPU v7x, 512 devices: a whole 4x8x8 slice. The times are simulated.
512 devices in a mesh: gx: 16 (over z, core), gy: 8 (over y), gz: 4 (over x).
Axes of the slice: x: 4, y: 8, z: 8, core: 2. Of those that a mesh axis runs over, the one named last changes fastest.
Arguments:
- start: float32 [4, 80, 256, 512], P(None, 'gx', 'gy', 'gz'), may hold values from -6 to 6
- rhs_block: float32 [4, 80, 256, 512], P(None, 'gx', 'gy', 'gz'), may hold values from -6 to 6
- coefficients: float32 [4, 80, 256, 512], P(None, 'gx', 'gy', 'gz'), may hold values from 0.5 to 2
Outputs:
- solution: float32 [4, 80, 256, 512], P(None, 'gx', 'gy', 'gz')
All inputs are finite; a program needn't handle non-finite values.
Results may differ from a plain program's by a relative error of at most 0.0003.
Values sent between devices are 32-bit elements; how exact they have to be, the bound alone decides.
A program may use at most 192 MiB of HBM per device.

v0:
```python
import jax
import jax.numpy as jnp
from jax import lax
from jax.sharding import PartitionSpec as P

S = 4
basis_shift = 8.75
basis_scale = 4.0


def padded(block, sides, width):
    for axis, dim in sides:
        count = lax.axis_size(axis)
        forward = [(i, i + 1) for i in range(count - 1)]
        backward = [(target, source) for source, target in forward]
        low = lax.ppermute(
            lax.slice_in_dim(block, block.shape[dim] - width, None, axis=dim), axis, forward
        )
        high = lax.ppermute(lax.slice_in_dim(block, 0, width, axis=dim), axis, backward)
        block = jnp.concatenate([low, block, high], axis=dim)
    return block


def stencil(field, coefs):
    center = field[:, 1:-1, 1:-1, 1:-1]
    result = coefs[0, 1:-1, 1:-1, 1:-1] * center
    result = result + coefs[1, 1:-1, 1:-1, 1:-1] * (center - field[:, 2:, 1:-1, 1:-1])
    result = result + coefs[1, :-2, 1:-1, 1:-1] * (center - field[:, :-2, 1:-1, 1:-1])
    result = result + coefs[2, 1:-1, 1:-1, 1:-1] * (center - field[:, 1:-1, 2:, 1:-1])
    result = result + coefs[2, 1:-1, :-2, 1:-1] * (center - field[:, 1:-1, :-2, 1:-1])
    result = result + coefs[3, 1:-1, 1:-1, 1:-1] * (center - field[:, 1:-1, 1:-1, 2:])
    result = result + coefs[3, 1:-1, 1:-1, :-2] * (center - field[:, 1:-1, 1:-1, :-2])
    return result


def reflect_rows(tall):
    count = tall.shape[0]
    entries = tall.shape[1]
    position = jnp.arange(entries)
    for j in range(count):
        column = jnp.where(position >= j, tall[j], 0.0)
        length = jnp.sqrt(jnp.sum(column * column))
        leading = tall[j, j]
        mirror = -jnp.where(leading >= 0, 1.0, -1.0) * length
        vector = column - mirror * (position == j).astype(jnp.float32)
        weight = jnp.sum(vector * vector)
        project = jnp.dot(tall, vector, precision=lax.Precision.HIGHEST) / weight
        tall = tall - 2.0 * project[:, None] * vector[None, :]
    factor = tall.T
    flip_sign = jnp.where(jnp.diagonal(factor) >= 0, 1.0, -1.0)
    return jnp.triu(factor * flip_sign[:, None])


def back_solve(triangle, values):
    count = triangle.shape[0]
    answer = [None] * count
    for i in reversed(range(count)):
        partial_sum = values[i]
        for j in range(i + 1, count):
            partial_sum = partial_sum - triangle[i, j] * answer[j]
        answer[i] = partial_sum / triangle[i, i]
    return jnp.stack(answer)


def least_squares(upper, nrhs):
    total = upper.shape[0]
    kept = total - nrhs
    rows = jnp.arange(total)[:, None]
    cols = jnp.arange(kept)[None, :]
    shifts = basis_shift * (rows == cols).astype(jnp.float32) + basis_scale * (
        rows == cols + nrhs
    ).astype(jnp.float32)
    mixed = jnp.dot(upper, shifts, precision=lax.Precision.HIGHEST)
    joined = jnp.concatenate([mixed, upper[:, :nrhs]], axis=1)
    reduced = reflect_rows(joined.T)
    return back_solve(reduced[:kept, :kept], reduced[:kept, kept:])


def local(start, rhs_block, coefficients):
    nrhs = start.shape[0]
    guess_ext, coef_ext = (
        padded(start, (("gx", 1), ("gy", 2), ("gz", 3)), 1),
        padded(coefficients, (("gx", 1), ("gy", 2), ("gz", 3)), 1),
    )
    blocks = [rhs_block - stencil(guess_ext, coef_ext)]
    for step in range(S):
        before = blocks[-1]
        widened = padded(before, (("gx", 1), ("gy", 2), ("gz", 3)), 1)
        blocks.append((stencil(widened, coef_ext) - basis_shift * before) / basis_scale)
    tall = jnp.stack(blocks).reshape(len(blocks) * nrhs, -1)
    local_gram = jnp.dot(tall, tall.T, precision=lax.Precision.HIGHEST)
    gram = lax.psum(local_gram, ("gx", "gy", "gz"))
    upper = jnp.linalg.cholesky(gram).T
    weights = least_squares(upper, nrhs)
    kept = tall.shape[0] - nrhs
    update = jnp.dot(weights.T, tall[:kept], precision=lax.Precision.HIGHEST)
    return start + update.reshape(start.shape)


def solution(mesh):
    placed = (P(None, "gx", "gy", "gz"), P(None, "gx", "gy", "gz"), P(None, "gx", "gy", "gz"))
    return jax.shard_map(
        local, mesh=mesh, in_specs=placed, out_specs=P(None, "gx", "gy", "gz"), check_vma=False
    )
```

profile of v0, /device:TPU:1, one launch (start us, length us, event | category | flops | bytes accessed | tf_op | source)
XLA Modules:
  0.0 541.6 jit_solution(3785583033890651326)
XLA Ops:
  0.9 5.5 %collective-permute-start.1 = (f32[4,1,32,128]{3,2,1,0:T(8,128)S(1)}, f32[4,1,32,128]{3,2,1,0:T(8,128)S(1)}, u32[]{:S(2)}, u32[]{:S(2)}) collective-permute-start(f32[4,1,32,128]{3,2,1,0:T(8,128)S(1)} %get-tuple-element.80), channel_id=1, source_target_pairs={{0,32},{32,64},{64,96},{96,128},{128,160},{160,192},{192,224},{224... | collective-permute-start | bytes 196616 | tf_op jit(solution)/shard_map/ppermute | solution.py:16
  6.5 4.7 collective-permute-start.4
  12.1 1.9 collective-permute-start.2
  14.0 2.4 collective-permute-start
  18.4 1.7 collective-permute-start.5
  24.1 5.2 collective-permute-start.6
  29.4 1.8 copy.480
  31.2 2.0 copy.479
  33.2 1.9 copy.481
  36.0 3.1 collective-permute-start.9
  41.9 1.3 copy.476
  44.5 1.3 copy.483
  45.9 4.0 collective-permute-start.10
  50.8 2.4 fusion.42
  56.7 2.2 constant_dynamic-update-slice_fusion.9
  58.9 1.9 collective-permute-start.11
  60.8 5.3 collective-permute-start.12
  66.2 1.3 collective-permute-done.12
  68.8 4.0 collective-permute-start.14
  74.9 1.3 copy.491
  77.5 1.3 copy.493
  78.9 4.0 collective-permute-start.16
  85.1 1.6 constant_dynamic-update-slice_fusion.8
  88.8 1.9 collective-permute-start.17
  90.7 6.2 %collective-permute-start.18 = (f32[4,1,32,128]{3,2,1,0:T(8,128)S(1)}, f32[4,1,32,128]{3,2,1,0:T(8,128)S(1)}, u32[]{:S(2)}, u32[]{:S(2)}) collective-permute-start(f32[4,1,32,128]{3,2,1,0:T(8,128)S(1)} %get-tuple-element.70), channel_id=1, source_target_pairs={{0,32},{32,64},{64,96},{96,128},{128,160},{160,192},{192,224},{224... | collective-permute-start | bytes 196616 | tf_op jit(solution)/shard_map/ppermute | solution.py:16
  96.9 1.3 collective-permute-done.18
  99.6 4.5 collective-permute-start.20
  107.2 4.5 collective-permute-start.22
  115.3 1.9 collective-permute-start.23
  117.3 5.6 %collective-permute-start.24 = (f32[4,1,32,128]{3,2,1,0:T(8,128)S(1)}, f32[4,1,32,128]{3,2,1,0:T(8,128)S(1)}, u32[]{:S(2)}, u32[]{:S(2)}) collective-permute-start(f32[4,1,32,128]{3,2,1,0:T(8,128)S(1)} %get-tuple-element.68), channel_id=1, source_target_pairs={{0,32},{32,64},{64,96},{96,128},{128,160},{160,192},{192,224},{224... | collective-permute-start | bytes 196616 | tf_op jit(solution)/shard_map/ppermute | solution.py:16
  125.5 4.5 collective-permute-start.26
  133.1 4.5 collective-permute-start.28
  139.3 1.9 collective-permute-start.29
  141.2 6.0 %collective-permute-start.30 = (f32[4,1,32,128]{3,2,1,0:T(8,128)S(1)}, f32[4,1,32,128]{3,2,1,0:T(8,128)S(1)}, u32[]{:S(2)}, u32[]{:S(2)}) collective-permute-start(f32[4,1,32,128]{3,2,1,0:T(8,128)S(1)} %get-tuple-element.62), channel_id=1, source_target_pairs={{0,32},{32,64},{64,96},{96,128},{128,160},{160,192},{192,224},{224... | collective-permute-start | bytes 196616 | tf_op jit(solution)/shard_map/ppermute | solution.py:16
  149.9 5.5 %collective-permute-start.32 = (f32[4,7,1,128]{3,0,2,1:T(4,128)S(1)}, f32[4,7,1,128]{3,0,2,1:T(4,128)S(1)}, u32[]{:S(2)}, u32[]{:S(2)}) collective-permute-start(f32[4,7,1,128]{3,0,2,1:T(4,128)S(1)} %copy.517), channel_id=1, source_target_pairs={{0,4},{4,8},{8,12},{12,16},{16,20},{20,24},{24,28},{1,5},{5,9},{9,... | collective-permute-start | bytes 43016 | tf_op jit(solution)/shard_map/ppermute | solution.py:16
  159.0 5.1 collective-permute-start.34
  165.3 1.3 slice.1287
  166.6 1.6 copy.552
  169.3 1.8 copy.524
  171.2 2.2 fusion.49
  173.5 1.7 reshape.530
  175.2 2.1 fusion.311
  177.3 116.5 %psum.7 = f32[20,20]{0,1:T(8,128)S(1)} all-reduce(f32[20,20]{0,1:T(8,128)S(1)} %fusion.311), channel_id=1, replica_groups=mesh['gx'=16,'gy'=8,'gz'=4] {'gx','gy','gz'}, use_global_device_ids=true, to_apply=%region_0.0 | all-reduce | flops 400 | bytes 3200 | tf_op jit(solution)/shard_map/psum | solution.py:92
  293.9 1.8 cholesky.19
  395.1 65.5 %subtract_divide_fusion = (f32[1,4]{1,0:T(1,128)S(1)}, f32[1,4]{1,0:T(1,128)S(1)}, f32[1,4]{1,0:T(1,128)S(1)}, f32[1,4]{1,0:T(1,128)S(1)}, f32[1,4]{1,0:T(1,128)...) fusion(f32[20,20]{1,0:T(8,128)S(1)} %multiply_select_fusion, ...), kind=kLoop, calls=%fused_computation.602 | loop fusion | flops 784 | bytes 884 | tf_op jit(solution)/shard_map/div | solution.py:61
  461.0 57.8 %fusion.191 = (f32[4]{0:T(128)S(1)}, f32[4]{0:T(128)S(1)}, f32[4]{0:T(128)S(1)}, f32[4]{0:T(128)S(1)}, f32[4]{0:T(128)S(1)}, /*index=5*/f32[4]{0:T(128)S(1)}, f3...) fusion(f32[20,20]{1,0:T(8,128)S(1)} %multiply_select_fusion, f32[1,4]{1,0:T(1,128)S(1)} %get-tuple-element.16, ...), kind=kLoop, calls=%fused_computation.504 | loop fusion | flops 704 | bytes 756 | tf_op jit(solution)/shard_map/div | solution.py:61
  518.8 19.3 %fusion.244 = (f32[1,4]{1,0:T(1,128)S(1)}, f32[4]{0:T(128)S(1)}) fusion(f32[1,4]{1,0:T(1,128)S(1)} %get-tuple-element.19, f32[1,4]{1,0:T(1,128)S(1)} %get-tuple-element.18, f32[1,4]{1,0:T(1,128)S(1)} %get-tuple-element.17, f32[1,4]{1,0:T(1,128)S(1)} %get-tuple-element.16, f32[4]{0:T(128)S(1)} %get-tuple-element.31, f32[4]{0:T(128)S(1)} %get-tuple-element.30, ...), kind=kLoop, calls=%fused_computation.656 | loop fusion | flops 240 | bytes 412 | tf_op jit(solution)/shard_map/stack | solution.py:62
  539.3 1.4 fusion
  (354 shorter events, 123.1 us)
Async XLA Ops:
  0.0 21.4 %copy-start.1 = (f32[4,5,32,128]{3,2,1,0:T(8,128)S(1)}, f32[4,5,32,128]{3,2,1,0:T(8,128)}, u32[]{:S(2)}) copy-start(f32[4,5,32,128]{3,2,1,0:T(8,128)} %param.3) | copy-start | bytes 983044
  0.9 28.4 %copy-start = (f32[4,5,32,128]{3,2,1,0:T(8,128)S(1)}, f32[4,5,32,128]{3,2,1,0:T(8,128)}, u32[]{:S(2)}) copy-start(f32[4,5,32,128]{3,2,1,0:T(8,128)} %param.5) | copy-start | bytes 983044
  0.9 15.5 %collective-permute-start.1 = (f32[4,1,32,128]{3,2,1,0:T(8,128)S(1)}, f32[4,1,32,128]{3,2,1,0:T(8,128)S(1)}, u32[]{:S(2)}, u32[]{:S(2)}) collective-permute-start(f32[4,1,32,128]{3,2,1,0:T(8,128)S(1)} %get-tuple-element.80), channel_id=1, source_target_pairs={{0,32},{32,64},{64,96},{96,128},{128,160},{160,192},{192,224},{224... | collective-permute-start | bytes 196616 | tf_op jit(solution)/shard_map/ppermute | solution.py:16
  6.5 11.0 %collective-permute-start.4 = (f32[4,1,32,128]{3,2,1,0:T(8,128)S(1)}, f32[4,1,32,128]{3,2,1,0:T(8,128)S(1)}, u32[]{:S(2)}, u32[]{:S(2)}) collective-permute-start(f32[4,1,32,128]{3,2,1,0:T(8,128)S(1)} %get-tuple-element.79), channel_id=1, source_target_pairs={{32,0},{64,32},{96,64},{128,96},{160,128},{192,160},{224,192},{256... | collective-permute-start | bytes 196616 | tf_op jit(solution)/shard_map/ppermute | solution.py:19
  12.1 9.3 %collective-permute-start.2 = (f32[4,1,32,128]{3,2,1,0:T(8,128)S(1)}, f32[4,1,32,128]{3,2,1,0:T(8,128)S(1)}, u32[]{:S(2)}, u32[]{:S(2)}) collective-permute-start(f32[4,1,32,128]{3,2,1,0:T(8,128)S(1)} %get-tuple-element.82), channel_id=1, source_target_pairs={{0,32},{32,64},{64,96},{96,128},{128,160},{160,192},{192,224},{224... | collective-permute-start | bytes 196616 | tf_op jit(solution)/shard_map/ppermute | solution.py:16
  14.0 7.5 %collective-permute-start = (f32[4,1,32,128]{3,2,1,0:T(8,128)S(1)}, f32[4,1,32,128]{3,2,1,0:T(8,128)S(1)}, u32[]{:S(2)}, u32[]{:S(2)}) collective-permute-start(f32[4,1,32,128]{3,2,1,0:T(8,128)S(1)} %get-tuple-element.81), channel_id=1, source_target_pairs={{32,0},{64,32},{96,64},{128,96},{160,128},{192,160},{224,192},{256... | collective-permute-start | bytes 196616 | tf_op jit(solution)/shard_map/ppermute | solution.py:19
  17.7 11.6 %copy-start.19 = (f32[4,7,32,128]{3,1,2,0:T(8,128)}, f32[4,7,32,128]{3,1,2,0:T(8,128)S(1)}, u32[]{:S(2)}) copy-start(f32[4,7,32,128]{3,1,2,0:T(8,128)S(1)} %copy.469) | copy-start | bytes 1376260
  18.4 12.8 %collective-permute-start.5 = (f32[4,7,1,128]{3,1,2,0:T(8,128)}, f32[4,7,1,128]{3,1,2,0:T(8,128)S(1)}, u32[]{:S(2)}, u32[]{:S(2)}) collective-permute-start(f32[4,7,1,128]{3,1,2,0:T(8,128)} %get-tuple-element.50), channel_id=1, source_target_pairs={{0,4},{4,8},{8,12},{12,16},{16,20},{20,24},{24,28},{1,5},{5,9},{9,... | collective-permute-start | bytes 43016 | tf_op jit(solution)/shard_map/ppermute | solution.py:16
  20.1 13.1 %collective-permute-start.8 = (f32[4,7,1,128]{3,1,2,0:T(8,128)}, f32[4,7,1,128]{3,1,2,0:T(8,128)S(1)}, u32[]{:S(2)}, u32[]{:S(2)}) collective-permute-start(f32[4,7,1,128]{3,1,2,0:T(8,128)} %get-tuple-element.51), channel_id=1, source_target_pairs={{4,0},{8,4},{12,8},{16,12},{20,16},{24,20},{28,24},{5,1},{9,5},{13... | collective-permute-start | bytes 43016 | tf_op jit(solution)/shard_map/ppermute | solution.py:19
  22.2 16.9 %collective-permute-start.3 = (f32[4,7,1,128]{3,0,2,1:T(4,128)}, f32[4,7,1,128]{3,0,2,1:T(4,128)}, u32[]{:S(2)}, u32[]{:S(2)}) collective-permute-start(f32[4,7,1,128]{3,0,2,1:T(4,128)} %copy.550), channel_id=1, source_target_pairs={{4,0},{8,4},{12,8},{16,12},{20,16},{24,20},{28,24},{5,1},{9,5},{13... | collective-permute-start | bytes 43016 | tf_op jit(solution)/shard_map/ppermute | solution.py:19
  24.1 15.8 %collective-permute-start.6 = (f32[4,7,1,128]{3,0,2,1:T(4,128)}, f32[4,7,1,128]{3,0,2,1:T(4,128)}, u32[]{:S(2)}, u32[]{:S(2)}) collective-permute-start(f32[4,7,1,128]{3,0,2,1:T(4,128)} %copy.551), channel_id=1, source_target_pairs={{0,4},{4,8},{8,12},{12,16},{16,20},{20,24},{24,28},{1,5},{5,9},{9,... | collective-permute-start | bytes 43016 | tf_op jit(solution)/shard_map/ppermute | solution.py:16
  29.4 55.7 %copy-start.5 = (f32[5,32,128]{2,1,0:T(8,128)}, f32[5,32,128]{2,1,0:T(8,128)S(1)}, u32[]{:S(2)}) copy-start(f32[5,32,128]{2,1,0:T(8,128)S(1)} %get-tuple-element.77) | copy-start | bytes 245764
  29.4 55.7 %copy-start.8 = (f32[5,32,128]{2,1,0:T(8,128)}, f32[5,32,128]{2,1,0:T(8,128)S(1)}, u32[]{:S(2)}) copy-start(f32[5,32,128]{2,1,0:T(8,128)S(1)} %get-tuple-element.78) | copy-start | bytes 245764
  29.4 109.4 %copy-start.3 = (f32[5,32,128]{2,1,0:T(8,128)}, f32[5,32,128]{2,1,0:T(8,128)S(1)}, u32[]{:S(2)}) copy-start(f32[5,32,128]{2,1,0:T(8,128)S(1)} %get-tuple-element.76) | copy-start | bytes 245764
  36.0 14.8 %collective-permute-start.9 = (f32[4,7,34,1]{2,1,3,0:T(8,128)S(1)}, f32[4,7,34,1]{2,1,3,0:T(8,128)S(1)}, u32[]{:S(2)}, u32[]{:S(2)}) collective-permute-start(f32[4,7,34,1]{2,1,3,0:T(8,128)S(1)} %pad_maximum_fusion.93), channel_id=1, source_target_pairs={{0,1},{1,2},{2,3},{4,5},{5,6},{6,7},{8,9},{9,10},{10,11},{12,13},{... | collective-permute-start | bytes 11432 | tf_op jit(solution)/shard_map/ppermute | solution.py:16
  43.2 11.2 %collective-permute-start.7 = (f32[4,7,34,1]{2,0,3,1:T(4,128)S(1)}, f32[4,7,34,1]{2,0,3,1:T(4,128)S(1)}, u32[]{:S(2)}, u32[]{:S(2)}) collective-permute-start(f32[4,7,34,1]{2,0,3,1:T(4,128)S(1)} %copy.476), channel_id=1, source_target_pairs={{1,0},{2,1},{3,2},{5,4},{6,5},{7,6},{9,8},{10,9},{11,10},{13,12},{... | collective-permute-start | bytes 11432 | tf_op jit(solution)/shard_map/ppermute | solution.py:19
  45.9 9.7 %collective-permute-start.10 = (f32[4,7,34,1]{2,0,3,1:T(4,128)S(1)}, f32[4,7,34,1]{2,0,3,1:T(4,128)S(1)}, u32[]{:S(2)}, u32[]{:S(2)}) collective-permute-start(f32[4,7,34,1]{2,0,3,1:T(4,128)S(1)} %copy.483), channel_id=1, source_target_pairs={{0,1},{1,2},{2,3},{4,5},{5,6},{6,7},{8,9},{9,10},{10,11},{12,13},{... | collective-permute-start | bytes 11432 | tf_op jit(solution)/shard_map/ppermute | solution.py:16
  50.8 34.3 %copy-start.11 = (f32[5,32,128]{2,1,0:T(8,128)}, f32[5,32,128]{2,1,0:T(8,128)S(1)}, u32[]{:S(2)}) copy-start(f32[5,32,128]{2,1,0:T(8,128)S(1)} %copy.471) | copy-start | bytes 245764
  54.4 84.4 %copy-start.14 = (f32[5,32,128]{2,1,0:T(8,128)}, f32[5,32,128]{2,1,0:T(8,128)S(1)}, u32[]{:S(2)}) copy-start(f32[5,32,128]{2,1,0:T(8,128)S(1)} %copy.482) | copy-start | bytes 245764
  58.9 7.3 %collective-permute-start.11 = (f32[4,1,32,128]{3,2,1,0:T(8,128)S(1)}, f32[4,1,32,128]{3,2,1,0:T(8,128)S(1)}, u32[]{:S(2)}, u32[]{:S(2)}) collective-permute-start(f32[4,1,32,128]{3,2,1,0:T(8,128)S(1)} %get-tuple-element.73), channel_id=1, source_target_pairs={{32,0},{64,32},{96,64},{128,96},{160,128},{192,160},{224,192},{256... | collective-permute-start | bytes 196616 | tf_op jit(solution)/shard_map/ppermute | solution.py:19
  60.8 6.6 %collective-permute-start.12 = (f32[4,1,32,128]{3,2,1,0:T(8,128)S(1)}, f32[4,1,32,128]{3,2,1,0:T(8,128)S(1)}, u32[]{:S(2)}, u32[]{:S(2)}) collective-permute-start(f32[4,1,32,128]{3,2,1,0:T(8,128)S(1)} %get-tuple-element.72), channel_id=1, source_target_pairs={{0,32},{32,64},{64,96},{96,128},{128,160},{160,192},{192,224},{224... | collective-permute-start | bytes 196616 | tf_op jit(solution)/shard_map/ppermute | solution.py:16
  67.5 5.3 collective-permute-start.13
  68.8 4.8 collective-permute-start.14
  76.2 6.6 %collective-permute-start.15 = (f32[4,7,34,1]{2,0,3,1:T(4,128)S(1)}, f32[4,7,34,1]{2,0,3,1:T(4,128)S(1)}, u32[]{:S(2)}, u32[]{:S(2)}) collective-permute-start(f32[4,7,34,1]{2,0,3,1:T(4,128)S(1)} %copy.491), channel_id=1, source_target_pairs={{1,0},{2,1},{3,2},{5,4},{6,5},{7,6},{9,8},{10,9},{11,10},{13,12},{... | collective-permute-start | bytes 11432 | tf_op jit(solution)/shard_map/ppermute | solution.py:19
  78.9 5.1 collective-permute-start.16
  88.8 8.2 %collective-permute-start.17 = (f32[4,1,32,128]{3,2,1,0:T(8,128)S(1)}, f32[4,1,32,128]{3,2,1,0:T(8,128)S(1)}, u32[]{:S(2)}, u32[]{:S(2)}) collective-permute-start(f32[4,1,32,128]{3,2,1,0:T(8,128)S(1)} %get-tuple-element.71), channel_id=1, source_target_pairs={{32,0},{64,32},{96,64},{128,96},{160,128},{192,160},{224,192},{256... | collective-permute-start | bytes 196616 | tf_op jit(solution)/shard_map/ppermute | solution.py:19
  90.7 7.5 %collective-permute-start.18 = (f32[4,1,32,128]{3,2,1,0:T(8,128)S(1)}, f32[4,1,32,128]{3,2,1,0:T(8,128)S(1)}, u32[]{:S(2)}, u32[]{:S(2)}) collective-permute-start(f32[4,1,32,128]{3,2,1,0:T(8,128)S(1)} %get-tuple-element.70), channel_id=1, source_target_pairs={{0,32},{32,64},{64,96},{96,128},{128,160},{160,192},{192,224},{224... | collective-permute-start | bytes 196616 | tf_op jit(solution)/shard_map/ppermute | solution.py:16
  98.3 5.9 %collective-permute-start.19 = (f32[4,7,1,128]{3,0,2,1:T(4,128)S(1)}, f32[4,7,1,128]{3,0,2,1:T(4,128)S(1)}, u32[]{:S(2)}, u32[]{:S(2)}) collective-permute-start(f32[4,7,1,128]{3,0,2,1:T(4,128)S(1)} %copy.495), channel_id=1, source_target_pairs={{4,0},{8,4},{12,8},{16,12},{20,16},{24,20},{28,24},{5,1},{9,5},{13... | collective-permute-start | bytes 43016 | tf_op jit(solution)/shard_map/ppermute | solution.py:19
  99.6 5.4 collective-permute-start.20
  105.3 8.0 %copy-start.6 = (f32[5,32,128]{2,1,0:T(8,128)S(1)}, f32[5,32,128]{2,1,0:T(8,128)}, u32[]{:S(2)}) copy-start(f32[5,32,128]{2,1,0:T(8,128)} %copy-done.5) | copy-start | bytes 245764
  105.3 8.0 %copy-start.9 = (f32[5,32,128]{2,1,0:T(8,128)S(1)}, f32[5,32,128]{2,1,0:T(8,128)}, u32[]{:S(2)}) copy-start(f32[5,32,128]{2,1,0:T(8,128)} %copy-done.8) | copy-start | bytes 245764
  105.3 8.0 %copy-start.12 = (f32[5,32,128]{2,1,0:T(8,128)S(1)}, f32[5,32,128]{2,1,0:T(8,128)}, u32[]{:S(2)}) copy-start(f32[5,32,128]{2,1,0:T(8,128)} %copy-done.11) | copy-start | bytes 245764
  105.6 7.0 %collective-permute-start.21 = (f32[4,7,34,1]{2,0,3,1:T(4,128)S(1)}, f32[4,7,34,1]{2,0,3,1:T(4,128)S(1)}, u32[]{:S(2)}, u32[]{:S(2)}) collective-permute-start(f32[4,7,34,1]{2,0,3,1:T(4,128)S(1)} %copy.501), channel_id=1, source_target_pairs={{1,0},{2,1},{3,2},{5,4},{6,5},{7,6},{9,8},{10,9},{11,10},{13,12},{... | collective-permute-start | bytes 11432 | tf_op jit(solution)/shard_map/ppermute | solution.py:19
  107.2 5.8 %collective-permute-start.22 = (f32[4,7,34,1]{2,0,3,1:T(4,128)S(1)}, f32[4,7,34,1]{2,0,3,1:T(4,128)S(1)}, u32[]{:S(2)}, u32[]{:S(2)}) collective-permute-start(f32[4,7,34,1]{2,0,3,1:T(4,128)S(1)} %copy.503), channel_id=1, source_target_pairs={{0,1},{1,2},{2,3},{4,5},{5,6},{6,7},{8,9},{9,10},{10,11},{12,13},{... | collective-permute-start | bytes 11432 | tf_op jit(solution)/shard_map/ppermute | solution.py:16
  112.6 26.2 %copy-start.21 = (f32[5,32,128]{2,1,0:T(8,128)}, f32[5,32,128]{2,1,0:T(8,128)S(1)}, u32[]{:S(2)}) copy-start(f32[5,32,128]{2,1,0:T(8,128)S(1)} %broadcast_multiply_fusion.3) | copy-start | bytes 245764
  115.3 7.5 %collective-permute-start.23 = (f32[4,1,32,128]{3,2,1,0:T(8,128)S(1)}, f32[4,1,32,128]{3,2,1,0:T(8,128)S(1)}, u32[]{:S(2)}, u32[]{:S(2)}) collective-permute-start(f32[4,1,32,128]{3,2,1,0:T(8,128)S(1)} %get-tuple-element.69), channel_id=1, source_target_pairs={{32,0},{64,32},{96,64},{128,96},{160,128},{192,160},{224,192},{256... | collective-permute-start | bytes 196616 | tf_op jit(solution)/shard_map/ppermute | solution.py:19
  117.3 6.9 %collective-permute-start.24 = (f32[4,1,32,128]{3,2,1,0:T(8,128)S(1)}, f32[4,1,32,128]{3,2,1,0:T(8,128)S(1)}, u32[]{:S(2)}, u32[]{:S(2)}) collective-permute-start(f32[4,1,32,128]{3,2,1,0:T(8,128)S(1)} %get-tuple-element.68), channel_id=1, source_target_pairs={{0,32},{32,64},{64,96},{96,128},{128,160},{160,192},{192,224},{224... | collective-permute-start | bytes 196616 | tf_op jit(solution)/shard_map/ppermute | solution.py:16
  124.2 5.9 %collective-permute-start.25 = (f32[4,7,1,128]{3,0,2,1:T(4,128)S(1)}, f32[4,7,1,128]{3,0,2,1:T(4,128)S(1)}, u32[]{:S(2)}, u32[]{:S(2)}) collective-permute-start(f32[4,7,1,128]{3,0,2,1:T(4,128)S(1)} %copy.505), channel_id=1, source_target_pairs={{4,0},{8,4},{12,8},{16,12},{20,16},{24,20},{28,24},{5,1},{9,5},{13... | collective-permute-start | bytes 43016 | tf_op jit(solution)/shard_map/ppermute | solution.py:19
  125.5 5.4 collective-permute-start.26
  131.5 6.1 %collective-permute-start.27 = (f32[4,7,34,1]{2,0,3,1:T(4,128)S(1)}, f32[4,7,34,1]{2,0,3,1:T(4,128)S(1)}, u32[]{:S(2)}, u32[]{:S(2)}) collective-permute-start(f32[4,7,34,1]{2,0,3,1:T(4,128)S(1)} %copy.511), channel_id=1, source_target_pairs={{1,0},{2,1},{3,2},{5,4},{6,5},{7,6},{9,8},{10,9},{11,10},{13,12},{... | collective-permute-start | bytes 11432 | tf_op jit(solution)/shard_map/ppermute | solution.py:19
  133.1 5.4 collective-permute-start.28
  139.3 7.9 %collective-permute-start.29 = (f32[4,1,32,128]{3,2,1,0:T(8,128)S(1)}, f32[4,1,32,128]{3,2,1,0:T(8,128)S(1)}, u32[]{:S(2)}, u32[]{:S(2)}) collective-permute-start(f32[4,1,32,128]{3,2,1,0:T(8,128)S(1)} %get-tuple-element.63), channel_id=1, source_target_pairs={{32,0},{64,32},{96,64},{128,96},{160,128},{192,160},{224,192},{256... | collective-permute-start | bytes 196616 | tf_op jit(solution)/shard_map/ppermute | solution.py:19
  141.2 7.3 %collective-permute-start.30 = (f32[4,1,32,128]{3,2,1,0:T(8,128)S(1)}, f32[4,1,32,128]{3,2,1,0:T(8,128)S(1)}, u32[]{:S(2)}, u32[]{:S(2)}) collective-permute-start(f32[4,1,32,128]{3,2,1,0:T(8,128)S(1)} %get-tuple-element.62), channel_id=1, source_target_pairs={{0,32},{32,64},{64,96},{96,128},{128,160},{160,192},{192,224},{224... | collective-permute-start | bytes 196616 | tf_op jit(solution)/shard_map/ppermute | solution.py:16
  148.6 7.5 %collective-permute-start.31 = (f32[4,7,1,128]{3,0,2,1:T(4,128)S(1)}, f32[4,7,1,128]{3,0,2,1:T(4,128)S(1)}, u32[]{:S(2)}, u32[]{:S(2)}) collective-permute-start(f32[4,7,1,128]{3,0,2,1:T(4,128)S(1)} %copy.515), channel_id=1, source_target_pairs={{4,0},{8,4},{12,8},{16,12},{20,16},{24,20},{28,24},{5,1},{9,5},{13... | collective-permute-start | bytes 43016 | tf_op jit(solution)/shard_map/ppermute | solution.py:19
  149.9 6.3 %collective-permute-start.32 = (f32[4,7,1,128]{3,0,2,1:T(4,128)S(1)}, f32[4,7,1,128]{3,0,2,1:T(4,128)S(1)}, u32[]{:S(2)}, u32[]{:S(2)}) collective-permute-start(f32[4,7,1,128]{3,0,2,1:T(4,128)S(1)} %copy.517), channel_id=1, source_target_pairs={{0,4},{4,8},{8,12},{12,16},{16,20},{20,24},{24,28},{1,5},{5,9},{9,... | collective-permute-start | bytes 43016 | tf_op jit(solution)/shard_map/ppermute | solution.py:16
  156.8 11.5 %collective-permute-start.33 = (f32[4,7,34,1]{2,0,3,1:T(4,128)S(1)}, f32[4,7,34,1]{2,0,3,1:T(4,128)}, u32[]{:S(2)}, u32[]{:S(2)}) collective-permute-start(f32[4,7,34,1]{2,0,3,1:T(4,128)S(1)} %copy.521), channel_id=1, source_target_pairs={{1,0},{2,1},{3,2},{5,4},{6,5},{7,6},{9,8},{10,9},{11,10},{13,12},{... | collective-permute-start | bytes 11432 | tf_op jit(solution)/shard_map/ppermute | solution.py:19
  159.0 10.4 %collective-permute-start.34 = (f32[4,7,34,1]{2,0,3,1:T(4,128)}, f32[4,7,34,1]{2,0,3,1:T(4,128)}, u32[]{:S(2)}, u32[]{:S(2)}) collective-permute-start(f32[4,7,34,1]{2,0,3,1:T(4,128)} %copy.523), channel_id=1, source_target_pairs={{0,1},{1,2},{2,3},{4,5},{5,6},{6,7},{8,9},{9,10},{10,11},{12,13},{... | collective-permute-start | bytes 11432 | tf_op jit(solution)/shard_map/ppermute | solution.py:16
  384.5 156.3 %copy-start.2 = (f32[4,5,32,128]{3,2,1,0:T(8,128)S(1)}, f32[4,5,32,128]{3,2,1,0:T(8,128)}, u32[]{:S(2)}) copy-start(f32[4,5,32,128]{3,2,1,0:T(8,128)} %param.3) | copy-start | bytes 983044
  (13 other events, 50.2 us)
where the time goes:
time: 546 us; the launch traced here: 542 us
  other arithmetic  195 us (36%)
  blocking collectives  116 us (21%)
  starting transfers between devices  110 us (20%)
  local copies, waits for them, and re-layouts  62.4 us (11%)
  between operations  29.3 us (5%)
  matrix products  20.1 us (4%)
  waiting for transfers between devices  8.15 us (1%)
    div x2, other arithmetic, back_solve(): answer[i] = partial_sum / triangle[i, i]  123 us
    psum x1, blocking collectives, local(): gram = lax.psum(local_gram, ('gx', 'gy', 'gz'))  116 us
    ppermute x18, starting transfers between devices, padded(): lax.ppermute(lax.slice_in_dim(block, block.shape[dim] - width, None, axis...  81.2 us
    ppermute x17, starting transfers between devices, padded(): lax.ppermute(lax.slice_in_dim(block, 0, width, axis=dim), axis, backward)  28.9 us
    another operation x1, other arithmetic, back_solve(): return jnp.stack(answer)  19.3 us
    dot_general x20, matrix products, reflect_rows(): project = jnp.dot(tall, vector, precision=lax.Precision.HIGHEST) / weight  15.7 us
    reduce_sum x20, other arithmetic, reflect_rows(): length = jnp.sqrt(jnp.sum(column * column))  13.6 us
    reduce_sum x20, other arithmetic, reflect_rows(): weight = jnp.sum(vector * vector)  12 us
  transfers between devices with their start and end apart: 35, of which 8 were waited for; matrix products, arithmetic and copies ran while one was open for 6% of the time, Pallas kernels for 0%

commit v1 on v0

--- a/solution.py
+++ b/solution.py
@@ -89,7 +89,7 @@
         blocks.append((stencil(widened, coef_ext) - basis_shift * before) / basis_scale)
     tall = jnp.stack(blocks).reshape(len(blocks) * nrhs, -1)
     local_gram = jnp.dot(tall, tall.T, precision=lax.Precision.HIGHEST)
-    gram = lax.psum(local_gram, ("gx", "gy", "gz"))
+    gram = jnp.sum(lax.all_gather(local_gram, ("gx", "gy", "gz")), axis=0)
     upper = jnp.linalg.cholesky(gram).T
     weights = least_squares(upper, nrhs)
     kept = tall.shape[0] - nrhs

time: 546 us -> 596 us (1.092)
  blocking collectives: 116 us -> 168 us
  local copies, waits for them, and re-layouts: 62.4 us -> 53.7 us
    all_gather x0 -> x1, blocking collectives: none -> 168 us  [local(): gram = jnp.sum(lax.all_gather(local_gram, ('gx', 'gy', 'gz')), axis=0)]
    psum x1 -> x0, blocking collectives: 116 us -> none  [local(): gram = lax.psum(local_gram, ('gx', 'gy', 'gz'))]
  transfers between devices with their start and end apart: 35 -> 35, of which waited for: 8 -> 9; matrix products, arithmetic and copies ran while one was open for 6% -> 5% of each run, Pallas kernels for 0% -> 0%
where the time goes in v1:
time: 596 us; the launch traced here: 589 us
  other arithmetic  198 us (33%)
  blocking collectives  168 us (28%)
  starting transfers between devices  112 us (19%)
  local copies, waits for them, and re-layouts  53.7 us (9%)
  between operations  29.4 us (5%)
  matrix products  20.1 us (3%)
  waiting for transfers between devices  8.13 us (1%)
    all_gather x1, blocking collectives, local(): gram = jnp.sum(lax.all_gather(local_gram, ('gx', 'gy', 'gz')), axis=0)  168 us
    div x2, other arithmetic, back_solve(): answer[i] = partial_sum / triangle[i, i]  123 us
    ppermute x18, starting transfers between devices, padded(): lax.ppermute(lax.slice_in_dim(block, block.shape[dim] - width, None, axis...  82.7 us
    ppermute x17, starting transfers between devices, padded(): lax.ppermute(lax.slice_in_dim(block, 0, width, axis=dim), axis, backward)  28.9 us
    another operation x1, other arithmetic, back_solve(): return jnp.stack(answer)  19.3 us
    dot_general x20, matrix products, reflect_rows(): project = jnp.dot(tall, vector, precision=lax.Precision.HIGHEST) / weight  15.7 us
    reduce_sum x20, other arithmetic, reflect_rows(): length = jnp.sqrt(jnp.sum(column * column))  13.6 us
    reduce_sum x20, other arithmetic, reflect_rows(): weight = jnp.sum(vector * vector)  12 us
  transfers between devices with their start and end apart: 35, of which 9 were waited for; matrix products, arithmetic and copies ran while one was open for 5% of the time, Pallas kernels for 0%

profile of v1, /device:TPU:1, one launch (start us, length us, event | category | flops | bytes accessed | tf_op | source)
XLA Modules:
  0.0 588.7 jit_solution(14118948354361758518)
XLA Ops:
  0.9 5.5 collective-permute-start.1
  6.5 4.7 collective-permute-start.4
  12.1 1.9 collective-permute-start.2
  14.0 2.4 collective-permute-start
  17.8 1.7 collective-permute-start.5
  22.2 4.6 collective-permute-start.6
  26.9 1.8 copy.473
  28.8 1.9 copy.472
  30.7 2.0 copy.474
  32.7 1.5 pad_maximum_fusion.93
  34.2 3.7 collective-permute-start.9
  39.2 1.3 copy.469
  41.9 1.3 copy.476
  43.2 4.6 collective-permute-start.10
  48.7 1.6 fusion.42
  51.9 2.0 constant_dynamic-update-slice_fusion.9
  53.9 1.9 collective-permute-start.11
  55.9 5.3 collective-permute-start.12
  61.2 1.3 collective-permute-done.12
  63.9 4.3 collective-permute-start.14
  71.2 4.0 collective-permute-start.16
  78.3 1.9 collective-permute-start.17
  80.3 6.3 %collective-permute-start.18 = (f32[4,1,32,128]{3,2,1,0:T(8,128)S(1)}, f32[4,1,32,128]{3,2,1,0:T(8,128)S(1)}, u32[]{:S(2)}, u32[]{:S(2)}) collective-permute-start(f32[4,1,32,128]{3,2,1,0:T(8,128)S(1)} %get-tuple-element.70), channel_id=1, source_target_pairs={{0,32},{32,64},{64,96},{96,128},{128,160},{160,192},{192,224},{224... | collective-permute-start | bytes 196616 | tf_op jit(solution)/shard_map/ppermute | solution.py:16
  86.5 1.3 collective-permute-done.18
  89.2 4.5 collective-permute-start.20
  96.8 4.5 collective-permute-start.22
  105.0 1.9 collective-permute-start.23
  106.9 5.6 collective-permute-start.24
  115.1 5.1 collective-permute-start.26
  122.2 1.3 copy.504
  125.1 4.5 collective-permute-start.28
  131.3 1.9 collective-permute-start.29
  133.3 6.0 %collective-permute-start.30 = (f32[4,1,32,128]{3,2,1,0:T(8,128)S(1)}, f32[4,1,32,128]{3,2,1,0:T(8,128)S(1)}, u32[]{:S(2)}, u32[]{:S(2)}) collective-permute-start(f32[4,1,32,128]{3,2,1,0:T(8,128)S(1)} %get-tuple-element.62), channel_id=1, source_target_pairs={{0,32},{32,64},{64,96},{96,128},{128,160},{160,192},{192,224},{224... | collective-permute-start | bytes 196616 | tf_op jit(solution)/shard_map/ppermute | solution.py:16
  141.9 5.5 collective-permute-start.32
  151.6 5.1 collective-permute-start.34
  157.9 1.3 slice.1287
  159.3 1.6 copy.543
  161.9 1.8 copy.517
  163.8 2.3 fusion.49
  166.1 1.7 reshape.530
  167.8 2.1 convolution_bitcast_fusion
  170.0 167.6 %all-gather.1 = f32[512,20,20]{2,1,0:T(8,128)} all-gather(f32[1,20,20]{2,1,0:T(8,128)S(1)} %convolution_bitcast_fusion), channel_id=2, replica_groups=mesh['gx'=16,'gy'=8,'gz'=4] {'gx','gy','gz'}, dimensions={0}, use_global_device_ids=true | all-gather | bytes 820800 | tf_op jit(solution)/shard_map/all_gather | solution.py:92
  337.5 3.4 reduce_sum.369
  341.0 1.8 cholesky.19
  442.2 65.5 %subtract_divide_fusion = (f32[1,4]{1,0:T(1,128)S(1)}, f32[1,4]{1,0:T(1,128)S(1)}, f32[1,4]{1,0:T(1,128)S(1)}, f32[1,4]{1,0:T(1,128)S(1)}, f32[1,4]{1,0:T(1,128)...) fusion(f32[20,20]{1,0:T(8,128)S(1)} %multiply_select_fusion, ...), kind=kLoop, calls=%fused_computation.603 | loop fusion | flops 784 | bytes 884 | tf_op jit(solution)/shard_map/div | solution.py:61
  508.1 57.8 %fusion.191 = (f32[4]{0:T(128)S(1)}, f32[4]{0:T(128)S(1)}, f32[4]{0:T(128)S(1)}, f32[4]{0:T(128)S(1)}, f32[4]{0:T(128)S(1)}, /*index=5*/f32[4]{0:T(128)S(1)}, f3...) fusion(f32[20,20]{1,0:T(8,128)S(1)} %multiply_select_fusion, f32[1,4]{1,0:T(1,128)S(1)} %get-tuple-element.16, ...), kind=kLoop, calls=%fused_computation.505 | loop fusion | flops 704 | bytes 756 | tf_op jit(solution)/shard_map/div | solution.py:61
  565.9 19.3 %fusion.244 = (f32[1,4]{1,0:T(1,128)S(1)}, f32[4]{0:T(128)S(1)}) fusion(f32[1,4]{1,0:T(1,128)S(1)} %get-tuple-element.19, f32[1,4]{1,0:T(1,128)S(1)} %get-tuple-element.18, f32[1,4]{1,0:T(1,128)S(1)} %get-tuple-element.17, f32[1,4]{1,0:T(1,128)S(1)} %get-tuple-element.16, f32[4]{0:T(128)S(1)} %get-tuple-element.31, f32[4]{0:T(128)S(1)} %get-tuple-element.30, ...), kind=kLoop, calls=%fused_computation.657 | loop fusion | flops 240 | bytes 412 | tf_op jit(solution)/shard_map/stack | solution.py:62
  586.4 1.4 fusion
  (367 shorter events, 116.6 us)
Async XLA Ops:
  0.0 20.8 %copy-start.1 = (f32[4,5,32,128]{3,2,1,0:T(8,128)S(1)}, f32[4,5,32,128]{3,2,1,0:T(8,128)}, u32[]{:S(2)}) copy-start(f32[4,5,32,128]{3,2,1,0:T(8,128)} %param.3) | copy-start | bytes 983044
  0.9 25.9 %copy-start = (f32[4,5,32,128]{3,2,1,0:T(8,128)S(1)}, f32[4,5,32,128]{3,2,1,0:T(8,128)}, u32[]{:S(2)}) copy-start(f32[4,5,32,128]{3,2,1,0:T(8,128)} %param.5) | copy-start | bytes 983044
  0.9 15.5 %collective-permute-start.1 = (f32[4,1,32,128]{3,2,1,0:T(8,128)S(1)}, f32[4,1,32,128]{3,2,1,0:T(8,128)S(1)}, u32[]{:S(2)}, u32[]{:S(2)}) collective-permute-start(f32[4,1,32,128]{3,2,1,0:T(8,128)S(1)} %get-tuple-element.80), channel_id=1, source_target_pairs={{0,32},{32,64},{64,96},{96,128},{128,160},{160,192},{192,224},{224... | collective-permute-start | bytes 196616 | tf_op jit(solution)/shard_map/ppermute | solution.py:16
  6.5 11.0 %collective-permute-start.4 = (f32[4,1,32,128]{3,2,1,0:T(8,128)S(1)}, f32[4,1,32,128]{3,2,1,0:T(8,128)S(1)}, u32[]{:S(2)}, u32[]{:S(2)}) collective-permute-start(f32[4,1,32,128]{3,2,1,0:T(8,128)S(1)} %get-tuple-element.79), channel_id=1, source_target_pairs={{32,0},{64,32},{96,64},{128,96},{160,128},{192,160},{224,192},{256... | collective-permute-start | bytes 196616 | tf_op jit(solution)/shard_map/ppermute | solution.py:19
  12.1 8.7 %collective-permute-start.2 = (f32[4,1,32,128]{3,2,1,0:T(8,128)S(1)}, f32[4,1,32,128]{3,2,1,0:T(8,128)S(1)}, u32[]{:S(2)}, u32[]{:S(2)}) collective-permute-start(f32[4,1,32,128]{3,2,1,0:T(8,128)S(1)} %get-tuple-element.82), channel_id=1, source_target_pairs={{0,32},{32,64},{64,96},{96,128},{128,160},{160,192},{192,224},{224... | collective-permute-start | bytes 196616 | tf_op jit(solution)/shard_map/ppermute | solution.py:16
  14.0 6.8 %collective-permute-start = (f32[4,1,32,128]{3,2,1,0:T(8,128)S(1)}, f32[4,1,32,128]{3,2,1,0:T(8,128)S(1)}, u32[]{:S(2)}, u32[]{:S(2)}) collective-permute-start(f32[4,1,32,128]{3,2,1,0:T(8,128)S(1)} %get-tuple-element.81), channel_id=1, source_target_pairs={{32,0},{64,32},{96,64},{128,96},{160,128},{192,160},{224,192},{256... | collective-permute-start | bytes 196616 | tf_op jit(solution)/shard_map/ppermute | solution.py:19
  17.5 9.4 %copy-start.20 = (f32[4,7,32,128]{3,2,1,0:T(8,128)}, f32[4,7,32,128]{3,2,1,0:T(8,128)S(1)}, u32[]{:S(2)}) copy-start(f32[4,7,32,128]{3,2,1,0:T(8,128)S(1)} %constant_dynamic-update-slice_fusion.3) | copy-start | bytes 1376260
  17.7 9.1 %copy-start.19 = (f32[4,7,32,128]{3,1,2,0:T(8,128)}, f32[4,7,32,128]{3,1,2,0:T(8,128)S(1)}, u32[]{:S(2)}) copy-start(f32[4,7,32,128]{3,1,2,0:T(8,128)S(1)} %copy.462) | copy-start | bytes 1376260
  17.8 11.0 %collective-permute-start.5 = (f32[4,7,1,128]{3,1,2,0:T(8,128)S(1)}, f32[4,7,1,128]{3,1,2,0:T(8,128)S(1)}, u32[]{:S(2)}, u32[]{:S(2)}) collective-permute-start(f32[4,7,1,128]{3,1,2,0:T(8,128)S(1)} %get-tuple-element.50), channel_id=1, source_target_pairs={{0,4},{4,8},{8,12},{12,16},{16,20},{20,24},{24,28},{1,5},{5,9},{9,... | collective-permute-start | bytes 43016 | tf_op jit(solution)/shard_map/ppermute | solution.py:16
  19.4 11.3 %collective-permute-start.8 = (f32[4,7,1,128]{3,1,2,0:T(8,128)S(1)}, f32[4,7,1,128]{3,1,2,0:T(8,128)S(1)}, u32[]{:S(2)}, u32[]{:S(2)}) collective-permute-start(f32[4,7,1,128]{3,1,2,0:T(8,128)S(1)} %get-tuple-element.51), channel_id=1, source_target_pairs={{4,0},{8,4},{12,8},{16,12},{20,16},{24,20},{28,24},{5,1},{9,5},{13... | collective-permute-start | bytes 43016 | tf_op jit(solution)/shard_map/ppermute | solution.py:19
  20.9 17.0 %collective-permute-start.3 = (f32[4,7,1,128]{3,0,2,1:T(4,128)S(1)}, f32[4,7,1,128]{3,0,2,1:T(4,128)S(1)}, u32[]{:S(2)}, u32[]{:S(2)}) collective-permute-start(f32[4,7,1,128]{3,0,2,1:T(4,128)S(1)} %copy.541), channel_id=1, source_target_pairs={{4,0},{8,4},{12,8},{16,12},{20,16},{24,20},{28,24},{5,1},{9,5},{13... | collective-permute-start | bytes 43016 | tf_op jit(solution)/shard_map/ppermute | solution.py:19
  22.2 15.7 %collective-permute-start.6 = (f32[4,7,1,128]{3,0,2,1:T(4,128)S(1)}, f32[4,7,1,128]{3,0,2,1:T(4,128)S(1)}, u32[]{:S(2)}, u32[]{:S(2)}) collective-permute-start(f32[4,7,1,128]{3,0,2,1:T(4,128)S(1)} %copy.542), channel_id=1, source_target_pairs={{0,4},{4,8},{8,12},{12,16},{16,20},{20,24},{24,28},{1,5},{5,9},{9,... | collective-permute-start | bytes 43016 | tf_op jit(solution)/shard_map/ppermute | solution.py:16
  26.9 49.4 %copy-start.5 = (f32[5,32,128]{2,1,0:T(8,128)}, f32[5,32,128]{2,1,0:T(8,128)S(1)}, u32[]{:S(2)}) copy-start(f32[5,32,128]{2,1,0:T(8,128)S(1)} %get-tuple-element.77) | copy-start | bytes 245764
  26.9 49.4 %copy-start.8 = (f32[5,32,128]{2,1,0:T(8,128)}, f32[5,32,128]{2,1,0:T(8,128)S(1)}, u32[]{:S(2)}) copy-start(f32[5,32,128]{2,1,0:T(8,128)S(1)} %get-tuple-element.78) | copy-start | bytes 245764
  26.9 103.8 %copy-start.3 = (f32[5,32,128]{2,1,0:T(8,128)}, f32[5,32,128]{2,1,0:T(8,128)S(1)}, u32[]{:S(2)}) copy-start(f32[5,32,128]{2,1,0:T(8,128)S(1)} %get-tuple-element.76) | copy-start | bytes 245764
  34.2 14.6 %collective-permute-start.9 = (f32[4,7,34,1]{2,1,3,0:T(8,128)}, f32[4,7,34,1]{2,1,3,0:T(8,128)}, u32[]{:S(2)}, u32[]{:S(2)}) collective-permute-start(f32[4,7,34,1]{2,1,3,0:T(8,128)} %pad_maximum_fusion.93), channel_id=1, source_target_pairs={{0,1},{1,2},{2,3},{4,5},{5,6},{6,7},{8,9},{9,10},{10,11},{12,13},{... | collective-permute-start | bytes 11432 | tf_op jit(solution)/shard_map/ppermute | solution.py:16
  40.6 10.0 %collective-permute-start.7 = (f32[4,7,34,1]{2,0,3,1:T(4,128)S(1)}, f32[4,7,34,1]{2,0,3,1:T(4,128)S(1)}, u32[]{:S(2)}, u32[]{:S(2)}) collective-permute-start(f32[4,7,34,1]{2,0,3,1:T(4,128)S(1)} %copy.469), channel_id=1, source_target_pairs={{1,0},{2,1},{3,2},{5,4},{6,5},{7,6},{9,8},{10,9},{11,10},{13,12},{... | collective-permute-start | bytes 11432 | tf_op jit(solution)/shard_map/ppermute | solution.py:19
  43.2 7.7 %collective-permute-start.10 = (f32[4,7,34,1]{2,0,3,1:T(4,128)S(1)}, f32[4,7,34,1]{2,0,3,1:T(4,128)}, u32[]{:S(2)}, u32[]{:S(2)}) collective-permute-start(f32[4,7,34,1]{2,0,3,1:T(4,128)S(1)} %copy.476), channel_id=1, source_target_pairs={{0,1},{1,2},{2,3},{4,5},{5,6},{6,7},{8,9},{9,10},{10,11},{12,13},{... | collective-permute-start | bytes 11432 | tf_op jit(solution)/shard_map/ppermute | solution.py:16
  48.7 27.6 %copy-start.11 = (f32[5,32,128]{2,1,0:T(8,128)}, f32[5,32,128]{2,1,0:T(8,128)S(1)}, u32[]{:S(2)}) copy-start(f32[5,32,128]{2,1,0:T(8,128)S(1)} %copy.464) | copy-start | bytes 245764
  50.5 80.3 %copy-start.14 = (f32[5,32,128]{2,1,0:T(8,128)}, f32[5,32,128]{2,1,0:T(8,128)S(1)}, u32[]{:S(2)}) copy-start(f32[5,32,128]{2,1,0:T(8,128)S(1)} %copy.475) | copy-start | bytes 245764
  53.9 7.3 %collective-permute-start.11 = (f32[4,1,32,128]{3,2,1,0:T(8,128)S(1)}, f32[4,1,32,128]{3,2,1,0:T(8,128)S(1)}, u32[]{:S(2)}, u32[]{:S(2)}) collective-permute-start(f32[4,1,32,128]{3,2,1,0:T(8,128)S(1)} %get-tuple-element.73), channel_id=1, source_target_pairs={{32,0},{64,32},{96,64},{128,96},{160,128},{192,160},{224,192},{256... | collective-permute-start | bytes 196616 | tf_op jit(solution)/shard_map/ppermute | solution.py:19
  55.9 6.6 %collective-permute-start.12 = (f32[4,1,32,128]{3,2,1,0:T(8,128)S(1)}, f32[4,1,32,128]{3,2,1,0:T(8,128)S(1)}, u32[]{:S(2)}, u32[]{:S(2)}) collective-permute-start(f32[4,1,32,128]{3,2,1,0:T(8,128)S(1)} %get-tuple-element.72), channel_id=1, source_target_pairs={{0,32},{32,64},{64,96},{96,128},{128,160},{160,192},{192,224},{224... | collective-permute-start | bytes 196616 | tf_op jit(solution)/shard_map/ppermute | solution.py:16
  62.6 5.6 collective-permute-start.13
  63.9 5.1 collective-permute-start.14
  69.6 5.6 collective-permute-start.15
  71.2 4.8 collective-permute-start.16
  78.3 8.2 %collective-permute-start.17 = (f32[4,1,32,128]{3,2,1,0:T(8,128)S(1)}, f32[4,1,32,128]{3,2,1,0:T(8,128)S(1)}, u32[]{:S(2)}, u32[]{:S(2)}) collective-permute-start(f32[4,1,32,128]{3,2,1,0:T(8,128)S(1)} %get-tuple-element.71), channel_id=1, source_target_pairs={{32,0},{64,32},{96,64},{128,96},{160,128},{192,160},{224,192},{256... | collective-permute-start | bytes 196616 | tf_op jit(solution)/shard_map/ppermute | solution.py:19
  80.3 7.6 %collective-permute-start.18 = (f32[4,1,32,128]{3,2,1,0:T(8,128)S(1)}, f32[4,1,32,128]{3,2,1,0:T(8,128)S(1)}, u32[]{:S(2)}, u32[]{:S(2)}) collective-permute-start(f32[4,1,32,128]{3,2,1,0:T(8,128)S(1)} %get-tuple-element.70), channel_id=1, source_target_pairs={{0,32},{32,64},{64,96},{96,128},{128,160},{160,192},{192,224},{224... | collective-permute-start | bytes 196616 | tf_op jit(solution)/shard_map/ppermute | solution.py:16
  87.9 5.9 collective-permute-start.19
  89.2 5.4 collective-permute-start.20
  94.9 8.0 %copy-start.6 = (f32[5,32,128]{2,1,0:T(8,128)S(1)}, f32[5,32,128]{2,1,0:T(8,128)}, u32[]{:S(2)}) copy-start(f32[5,32,128]{2,1,0:T(8,128)} %copy-done.5) | copy-start | bytes 245764
  94.9 8.0 %copy-start.9 = (f32[5,32,128]{2,1,0:T(8,128)S(1)}, f32[5,32,128]{2,1,0:T(8,128)}, u32[]{:S(2)}) copy-start(f32[5,32,128]{2,1,0:T(8,128)} %copy-done.8) | copy-start | bytes 245764
  95.2 7.0 %collective-permute-start.21 = (f32[4,7,34,1]{2,0,3,1:T(4,128)S(1)}, f32[4,7,34,1]{2,0,3,1:T(4,128)S(1)}, u32[]{:S(2)}, u32[]{:S(2)}) collective-permute-start(f32[4,7,34,1]{2,0,3,1:T(4,128)S(1)} %copy.494), channel_id=1, source_target_pairs={{1,0},{2,1},{3,2},{5,4},{6,5},{7,6},{9,8},{10,9},{11,10},{13,12},{... | collective-permute-start | bytes 11432 | tf_op jit(solution)/shard_map/ppermute | solution.py:19
  96.8 5.8 collective-permute-start.22
  102.2 28.6 %copy-start.21 = (f32[5,32,128]{2,1,0:T(8,128)}, f32[5,32,128]{2,1,0:T(8,128)S(1)}, u32[]{:S(2)}) copy-start(f32[5,32,128]{2,1,0:T(8,128)S(1)} %broadcast_multiply_fusion.3) | copy-start | bytes 245764
  105.0 8.0 %collective-permute-start.23 = (f32[4,1,32,128]{3,2,1,0:T(8,128)S(1)}, f32[4,1,32,128]{3,2,1,0:T(8,128)S(1)}, u32[]{:S(2)}, u32[]{:S(2)}) collective-permute-start(f32[4,1,32,128]{3,2,1,0:T(8,128)S(1)} %get-tuple-element.69), channel_id=1, source_target_pairs={{32,0},{64,32},{96,64},{128,96},{160,128},{192,160},{224,192},{256... | collective-permute-start | bytes 196616 | tf_op jit(solution)/shard_map/ppermute | solution.py:19
  106.9 6.9 %collective-permute-start.24 = (f32[4,1,32,128]{3,2,1,0:T(8,128)S(1)}, f32[4,1,32,128]{3,2,1,0:T(8,128)S(1)}, u32[]{:S(2)}, u32[]{:S(2)}) collective-permute-start(f32[4,1,32,128]{3,2,1,0:T(8,128)S(1)} %get-tuple-element.68), channel_id=1, source_target_pairs={{0,32},{32,64},{64,96},{96,128},{128,160},{160,192},{192,224},{224... | collective-permute-start | bytes 196616 | tf_op jit(solution)/shard_map/ppermute | solution.py:16
  113.8 6.4 %collective-permute-start.25 = (f32[4,7,1,128]{3,0,2,1:T(4,128)S(1)}, f32[4,7,1,128]{3,0,2,1:T(4,128)S(1)}, u32[]{:S(2)}, u32[]{:S(2)}) collective-permute-start(f32[4,7,1,128]{3,0,2,1:T(4,128)S(1)} %copy.498), channel_id=1, source_target_pairs={{4,0},{8,4},{12,8},{16,12},{20,16},{24,20},{28,24},{5,1},{9,5},{13... | collective-permute-start | bytes 43016 | tf_op jit(solution)/shard_map/ppermute | solution.py:19
  115.1 5.9 %collective-permute-start.26 = (f32[4,7,1,128]{3,0,2,1:T(4,128)S(1)}, f32[4,7,1,128]{3,0,2,1:T(4,128)S(1)}, u32[]{:S(2)}, u32[]{:S(2)}) collective-permute-start(f32[4,7,1,128]{3,0,2,1:T(4,128)S(1)} %copy.500), channel_id=1, source_target_pairs={{0,4},{4,8},{8,12},{12,16},{16,20},{20,24},{24,28},{1,5},{5,9},{9,... | collective-permute-start | bytes 43016 | tf_op jit(solution)/shard_map/ppermute | solution.py:16
  123.5 6.1 %collective-permute-start.27 = (f32[4,7,34,1]{2,0,3,1:T(4,128)S(1)}, f32[4,7,34,1]{2,0,3,1:T(4,128)S(1)}, u32[]{:S(2)}, u32[]{:S(2)}) collective-permute-start(f32[4,7,34,1]{2,0,3,1:T(4,128)S(1)} %copy.504), channel_id=1, source_target_pairs={{1,0},{2,1},{3,2},{5,4},{6,5},{7,6},{9,8},{10,9},{11,10},{13,12},{... | collective-permute-start | bytes 11432 | tf_op jit(solution)/shard_map/ppermute | solution.py:19
  125.1 5.4 collective-permute-start.28
  131.3 7.9 %collective-permute-start.29 = (f32[4,1,32,128]{3,2,1,0:T(8,128)S(1)}, f32[4,1,32,128]{3,2,1,0:T(8,128)S(1)}, u32[]{:S(2)}, u32[]{:S(2)}) collective-permute-start(f32[4,1,32,128]{3,2,1,0:T(8,128)S(1)} %get-tuple-element.63), channel_id=1, source_target_pairs={{32,0},{64,32},{96,64},{128,96},{160,128},{192,160},{224,192},{256... | collective-permute-start | bytes 196616 | tf_op jit(solution)/shard_map/ppermute | solution.py:19
  133.3 7.3 %collective-permute-start.30 = (f32[4,1,32,128]{3,2,1,0:T(8,128)S(1)}, f32[4,1,32,128]{3,2,1,0:T(8,128)S(1)}, u32[]{:S(2)}, u32[]{:S(2)}) collective-permute-start(f32[4,1,32,128]{3,2,1,0:T(8,128)S(1)} %get-tuple-element.62), channel_id=1, source_target_pairs={{0,32},{32,64},{64,96},{96,128},{128,160},{160,192},{192,224},{224... | collective-permute-start | bytes 196616 | tf_op jit(solution)/shard_map/ppermute | solution.py:16
  140.6 7.6 %collective-permute-start.31 = (f32[4,7,1,128]{3,0,2,1:T(4,128)S(1)}, f32[4,7,1,128]{3,0,2,1:T(4,128)S(1)}, u32[]{:S(2)}, u32[]{:S(2)}) collective-permute-start(f32[4,7,1,128]{3,0,2,1:T(4,128)S(1)} %copy.508), channel_id=1, source_target_pairs={{4,0},{8,4},{12,8},{16,12},{20,16},{24,20},{28,24},{5,1},{9,5},{13... | collective-permute-start | bytes 43016 | tf_op jit(solution)/shard_map/ppermute | solution.py:19
  141.9 6.3 %collective-permute-start.32 = (f32[4,7,1,128]{3,0,2,1:T(4,128)S(1)}, f32[4,7,1,128]{3,0,2,1:T(4,128)S(1)}, u32[]{:S(2)}, u32[]{:S(2)}) collective-permute-start(f32[4,7,1,128]{3,0,2,1:T(4,128)S(1)} %copy.510), channel_id=1, source_target_pairs={{0,4},{4,8},{8,12},{12,16},{16,20},{20,24},{24,28},{1,5},{5,9},{9,... | collective-permute-start | bytes 43016 | tf_op jit(solution)/shard_map/ppermute | solution.py:16
  149.4 11.5 %collective-permute-start.33 = (f32[4,7,34,1]{2,0,3,1:T(4,128)}, f32[4,7,34,1]{2,0,3,1:T(4,128)}, u32[]{:S(2)}, u32[]{:S(2)}) collective-permute-start(f32[4,7,34,1]{2,0,3,1:T(4,128)} %copy.514), channel_id=1, source_target_pairs={{1,0},{2,1},{3,2},{5,4},{6,5},{7,6},{9,8},{10,9},{11,10},{13,12},{... | collective-permute-start | bytes 11432 | tf_op jit(solution)/shard_map/ppermute | solution.py:19
  151.6 10.4 %collective-permute-start.34 = (f32[4,7,34,1]{2,0,3,1:T(4,128)}, f32[4,7,34,1]{2,0,3,1:T(4,128)}, u32[]{:S(2)}, u32[]{:S(2)}) collective-permute-start(f32[4,7,34,1]{2,0,3,1:T(4,128)} %copy.516), channel_id=1, source_target_pairs={{0,1},{1,2},{2,3},{4,5},{5,6},{6,7},{8,9},{9,10},{10,11},{12,13},{... | collective-permute-start | bytes 11432 | tf_op jit(solution)/shard_map/ppermute | solution.py:16
  431.6 156.3 %copy-start.2 = (f32[4,5,32,128]{3,2,1,0:T(8,128)S(1)}, f32[4,5,32,128]{3,2,1,0:T(8,128)}, u32[]{:S(2)}) copy-start(f32[4,5,32,128]{3,2,1,0:T(8,128)} %param.3) | copy-start | bytes 983044
  (19 other events, 78.0 us)
